TPU v7x, 32 devices: a whole 2x2x4 slice. The times are simulated.
32 devices in a mesh: rows: 8 (over z, x), dim: 4 (over y, core).
Axes of the slice: x: 2, y: 2, z: 4, core: 2. Of those that a mesh axis runs over, the one named last changes fastest.
Arguments:
- embeddings: float32 [64, 512, 128], P('rows', 'dim'), as said below
- prior: float32 [64, 512, 128], P('rows', 'dim'), may hold values from -9 to 9
- neighbours: int32 [64, 16], P('rows'), may hold values from 0 to 63, as said below
- seed_mask: int32 [8192], P('rows'), may hold values 0 or 1
- families: int32 [8192], P('rows'), may hold values from 0 to 511
Outputs:
- log_ratio: float32 [8192, 512], P(('rows', 'dim'))
Inputs may be any that keep to these rules, and one draw needn't show every extreme that they name: `neighbours`: each list names 16 different blocks. Together, the lists of the 8 blocks 8g to 8g + 7 of one group name exactly 2 different blocks of every group of 8 blocks. `embeddings`: each row has its own positive scale.
All inputs are finite; a program needn't handle non-finite values. No bound on the sum of `seed_mask` on one device may be relied on, other than what follows from the above.
Results may differ from a plain program's by a relative error of at most 0.00078.
Values may be sent and summed in bfloat16 or wider, within the bound.
A program may use at most 64 MiB of HBM per device.

v0:
```python
import jax
import jax.numpy as jnp
from jax import lax
from jax.sharding import PartitionSpec as P

ITERS = 3


sharpness = 16.0
seed_weight = 0.5
label_floor = 0.001
norm_eps = 1e-06


def shards(embeddings, prior, neighbours, seed_mask, families):
    groups = lax.axis_size("rows")
    splits = lax.axis_size("dim")
    member = lax.axis_index("dim")
    blocks = neighbours.shape[0]
    links = neighbours.shape[1]
    width = embeddings.shape[1]
    block_rows = embeddings.shape[2]
    fam_part = prior.shape[1]
    fam_all = fam_part * splits
    slots = blocks // 4
    owned = blocks // splits
    local_squares = jnp.sum(embeddings * embeddings, axis=1)
    raised_prior = jnp.exp(prior)
    local_total = jnp.sum(raised_prior, axis=1)
    squares, prior_total = lax.psum((local_squares, local_total), "dim")
    unit_blocks = embeddings * lax.rsqrt(squares + norm_eps)[:, None, :]
    labels = (raised_prior / prior_total[:, None, :]).astype(jnp.bfloat16)
    everything = groups * blocks
    hits = neighbours[:, :, None] == jnp.arange(everything, dtype=jnp.int32)[None, None, :]
    named = jnp.any(hits, axis=(0, 1)).reshape(groups, blocks)
    places = jnp.arange(blocks, dtype=jnp.int32)
    ranked = jnp.argsort(jnp.where(named, places[None, :], blocks + places[None, :]), axis=1)[
        :, :slots
    ]
    wanted = lax.all_to_all(ranked, "rows", split_axis=0, concat_axis=0, tiled=True)
    owner = neighbours // blocks
    within = neighbours % blocks
    owner_slots = ranked[owner]
    match = (owner_slots == within[:, :, None]).astype(jnp.int32)
    position = jnp.sum(match * jnp.arange(slots, dtype=jnp.int32)[None, None, :], axis=2)
    flat = owner * slots + position
    outgoing = unit_blocks[wanted]
    arrived = lax.all_to_all(outgoing, "rows", split_axis=0, concat_axis=0, tiled=True).reshape(
        groups * slots, width, block_rows
    )
    keys = arrived[flat]
    products = jnp.einsum(
        "qer,qlek->qrlk",
        unit_blocks,
        keys,
        precision=lax.Precision.HIGHEST,
        preferred_element_type=jnp.float32,
    )
    cosine = lax.psum_scatter(
        products.reshape(owned * lax.axis_size("dim"), block_rows, links * block_rows),
        "dim",
        scatter_dimension=0,
        tiled=True,
    )
    raised = jnp.exp(sharpness * (cosine - 1.0))
    weights = (raised / jnp.sum(raised, axis=2, keepdims=True)).astype(jnp.bfloat16)
    weights = weights.reshape(owned, block_rows, links, block_rows)
    first_row = member * owned * block_rows
    my_seeds = lax.dynamic_slice_in_dim(seed_mask, first_row, owned * block_rows, 0)
    my_families = lax.dynamic_slice_in_dim(families, first_row, owned * block_rows, 0)
    onehot = (my_families[:, None] == jnp.arange(fam_all, dtype=jnp.int32)[None, :]).astype(
        jnp.float32
    )
    seeds = (seed_weight * my_seeds.astype(jnp.float32)[:, None] * onehot).reshape(
        owned, block_rows, fam_all
    )
    shifted = seeds
    total = seeds
    for sweep in range(ITERS):
        sending = labels[wanted]
        came = lax.all_to_all(sending, "rows", split_axis=0, concat_axis=0, tiled=True).reshape(
            groups * slots, fam_part, block_rows
        )
        near = came[flat]
        gathered = lax.all_to_all(near, "dim", split_axis=0, concat_axis=2, tiled=True)
        mixed = (
            jnp.einsum("qrlk,qlfk->qrf", weights, gathered, preferred_element_type=jnp.float32)
            + seeds
        )
        shifted = mixed + label_floor
        squared = shifted * shifted
        total = jnp.sum(squared, axis=2, keepdims=True)
        if sweep + 1 < ITERS:
            fresh = jnp.transpose((squared / total).astype(jnp.bfloat16), (0, 2, 1))
            labels = lax.all_to_all(fresh, "dim", split_axis=1, concat_axis=0, tiled=True)
    result = 2.0 * jnp.log(shifted) - jnp.log(total) + jnp.log(jnp.float32(fam_all))
    return result.reshape(owned * block_rows, fam_all)


def solution(mesh):
    return jax.shard_map(
        shards,
        mesh=mesh,
        in_specs=(
            P("rows", "dim", None),
            P("rows", "dim", None),
            P("rows", None),
            P("rows"),
            P("rows"),
        ),
        out_specs=P(("rows", "dim"), None),
        check_vma=False,
    )
```

profile of v0, /device:TPU:11, one launch (start us, length us, event | category | flops | bytes accessed | tf_op | source)
XLA Modules:
  0.0 382.1 jit_solution(3803444706961446836)
XLA Ops:
  6.5 0.0 copy-start
  6.5 0.0 copy-start.4
  6.5 0.9 fusion.22
  7.4 0.1 reshape.87
  7.5 0.1 copy.55
  7.6 0.1 iota_select_fusion
  7.7 0.7 sort.17
  8.3 0.7 copy.56
  9.0 5.7 %all-to-all-start = ((s32[8,1,2]{2,1,0:T(1,128)}), s32[8,1,2]{2,1,0:T(1,128)S(1)}, u32[]{:S(2)}, u32[]{:S(2)}) async-start(s32[8,1,2]{2,1,0:T(1,128)} %bitcast.46), calls=%async_computation | async-start | bytes 8192 | tf_op jit(solution)/shard_map/all_to_all | solution.py:40
  14.6 1.3 multiply_reduce_fusion
  15.9 6.3 %all-reduce = (f32[8,128]{1,0:T(8,128)S(1)}, f32[8,128]{1,0:T(8,128)S(1)}) all-reduce(f32[8,128]{1,0:T(8,128)S(1)} %get-tuple-element.15, f32[8,128]{1,0:T(8,128)S(1)} %get-tuple-element.16), channel_id=1, replica_groups=mesh['rows'=8,'dim'=4] {'dim'}, use_global_device_ids=true, to_apply=%region_1.0 | all-reduce | flops 2048 | bytes 16384 | tf_op jit(solution)/shard_map/psum | solution.py:30
  22.3 1.1 broadcast_multiply_fusion
  23.4 0.0 all-to-all-done
  23.4 0.1 copy.59
  23.5 0.1 copy.60
  23.6 0.1 reshape.97
  23.7 1.6 gather_fusion
  25.3 5.4 %all-to-all-start.1 = ((f32[8,2,128,128]{3,2,1,0:T(8,128)}), f32[8,2,128,128]{3,2,1,0:T(8,128)S(1)}, u32[]{:S(2)}, u32[]{:S(2)}) async-start(f32[8,2,128,128]{3,2,1,0:T(8,128)} %bitcast.2), calls=%async_computation.1 | async-start | bytes 2097152 | tf_op jit(solution)/shard_map/all_to_all | solution.py:48
  30.7 0.0 reduce-scatter.2.cloned.1.call-start
  30.7 0.0 copy-done.4
  30.7 0.1 reshape.105
  30.8 1.3 gather_fusion.1
  32.1 0.3 select_reduce_fusion
  32.4 0.1 reshape.113
  32.5 21.3 %all-to-all-done.1 = f32[8,2,128,128]{3,2,1,0:T(8,128)S(1)} async-done(((f32[8,2,128,128]{3,2,1,0:T(8,128)}), f32[8,2,128,128]{3,2,1,0:T(8,128)S(1)}, u32[]{:S(2)}, u32[]{:S(2)}) %all-to-all-start.1) | async-done | bytes 1048608 | tf_op jit(solution)/shard_map/all_to_all | solution.py:48
  53.9 4.3 %gather_fusion.2 = f32[128,128,128]{2,1,0:T(8,128)} fusion(f32[16,128,128]{2,1,0:T(8,128)S(1)} %bitcast.85, s32[1024]{0:T(1024)S(1)} %pad_clamp_fusion), kind=kCustom, calls=%fused_computation.2 | custom fusion | bytes 16777728 | tf_op jit(solution)/shard_map/gather | solution.py:51
  58.2 9.1 %copy.61 = f32[8,16,128,128]{2,3,1,0:T(8,128)} copy(f32[8,16,128,128]{3,2,1,0:T(8,128)} %bitcast.90) | data formatting | bytes 16777216 | tf_op jit(solution)/shard_map/gather | solution.py:51
  67.3 10.9 %convolution_bitcast_fusion = f32[8,128,2048]{1,2,0:T(8,128)} fusion(f32[8,128,128]{2,1,0:T(8,128)S(1)} %broadcast_multiply_fusion, f32[8,128,2048]{1,2,0:T(8,128)} %bitcast.86), kind=kOutput, calls=%fused_computation.10 | convolution fusion | flops 3221225472 | bytes 17301504
  78.3 0.0 reduce-scatter.2.cloned.1.call-update
  78.3 1.0 copy-done.3
  79.3 0.1 divide_convert_fusion.1
  79.4 0.6 gather_fusion.3
  80.1 17.7 %all_to_all.122 = bf16[8,2,128,128]{3,2,1,0:T(8,128)(2,1)S(1)} all-to-all(bf16[8,2,128,128]{3,2,1,0:T(8,128)(2,1)S(1)} %bitcast.105), channel_id=1, replica_groups=mesh['rows'=8,'dim'=4] {'rows'}, dimensions={0} | all-to-all | bytes 1048576 | tf_op jit(solution)/shard_map/all_to_all | solution.py:81
  97.8 3.1 gather_fusion.4
  100.8 7.0 %all-to-all-start.3 = ((bf16[8,16,128,128]{3,2,1,0:T(8,128)(2,1)}), bf16[8,16,128,128]{3,2,1,0:T(8,128)(2,1)}, u32[]{:S(2)}, u32[]{:S(2)}) async-start(bf16[8,16,128,128]{3,2,1,0:T(8,128)(2,1)} %bitcast.96), calls=%async_computation.4 | async-start | bytes 8388608 | tf_op jit(solution)/shard_map/all_to_all | solution.py:85
  107.8 0.0 copy-done
  107.8 0.1 dynamic-slice_bitcast_fusion
  107.9 0.8 multiply_bitcast_fusion
  108.7 86.9 %all-to-all-done.3 = bf16[8,16,128,128]{3,2,1,0:T(8,128)(2,1)} async-done(((bf16[8,16,128,128]{3,2,1,0:T(8,128)(2,1)}), bf16[8,16,128,128]{3,2,1,0:T(8,128)(2,1)}, u32[]{:S(2)}, u32[]{:S(2)}) %all-to-all-start.3) | async-done | bytes 4194336 | tf_op jit(solution)/shard_map/all_to_all | solution.py:85
  195.6 4.7 %copy.62 = bf16[2,16,4,128,128]{4,3,2,1,0:T(8,128)(2,1)} copy(bf16[2,16,4,128,128]{4,3,1,0,2:T(8,128)(2,1)} %bitcast.15) | data formatting | bytes 8388608 | tf_op jit(solution)/shard_map/all_to_all | solution.py:85
  200.3 2.1 fusion.1
  202.4 2.0 divide_convert_fusion
  204.5 0.0 copy-done.2
  204.5 1.5 fusion.15
  206.0 0.2 fusion.20
  206.2 0.2 copy.64
  206.4 8.0 %all_to_all.123 = bf16[2,512,128]{2,0,1:T(2,128)(2,1)S(1)} all-to-all(bf16[2,512,128]{2,0,1:T(2,128)(2,1)S(1)} %copy.64), channel_id=1, replica_groups=mesh['rows'=8,'dim'=4] {'dim'}, dimensions={1} | all-to-all | bytes 524288 | tf_op jit(solution)/shard_map/all_to_all | solution.py:95
  214.4 0.6 gather_fusion.5
  215.1 16.5 %all_to_all.124 = bf16[8,2,128,128]{3,2,1,0:T(8,128)(2,1)S(1)} all-to-all(bf16[8,2,128,128]{3,2,1,0:T(8,128)(2,1)S(1)} %bitcast.106), channel_id=1, replica_groups=mesh['rows'=8,'dim'=4] {'rows'}, dimensions={0} | all-to-all | bytes 1048576 | tf_op jit(solution)/shard_map/all_to_all | solution.py:81
  231.5 3.0 gather_fusion.6
  234.5 53.3 %all_to_all.125 = bf16[8,16,128,128]{3,2,1,0:T(8,128)(2,1)S(1)} all-to-all(bf16[8,16,128,128]{3,2,1,0:T(8,128)(2,1)} %bitcast.98), channel_id=1, replica_groups=mesh['rows'=8,'dim'=4] {'dim'}, dimensions={0} | all-to-all | bytes 8388608 | tf_op jit(solution)/shard_map/all_to_all | solution.py:85
  287.9 0.6 copy.67
  288.4 1.5 fusion.18
  290.0 0.2 fusion.19
  290.2 0.2 copy.69
  290.4 8.4 %all_to_all.126 = bf16[2,512,128]{2,0,1:T(2,128)(2,1)S(1)} all-to-all(bf16[2,512,128]{2,0,1:T(2,128)(2,1)S(1)} %copy.69), channel_id=1, replica_groups=mesh['rows'=8,'dim'=4] {'dim'}, dimensions={1} | all-to-all | bytes 524288 | tf_op jit(solution)/shard_map/all_to_all | solution.py:95
  298.9 0.6 gather_fusion.7
  299.5 16.3 %all_to_all.127 = bf16[8,2,128,128]{3,2,1,0:T(8,128)(2,1)S(1)} all-to-all(bf16[8,2,128,128]{3,2,1,0:T(8,128)(2,1)S(1)} %bitcast.104), channel_id=1, replica_groups=mesh['rows'=8,'dim'=4] {'rows'}, dimensions={0} | all-to-all | bytes 1048576 | tf_op jit(solution)/shard_map/all_to_all | solution.py:81
  315.9 3.0 gather_fusion.8
  318.9 53.3 %all_to_all.128 = bf16[8,16,128,128]{3,2,1,0:T(8,128)(2,1)S(1)} all-to-all(bf16[8,16,128,128]{3,2,1,0:T(8,128)(2,1)} %bitcast.97), channel_id=1, replica_groups=mesh['rows'=8,'dim'=4] {'dim'}, dimensions={0} | all-to-all | bytes 8388608 | tf_op jit(solution)/shard_map/all_to_all | solution.py:85
  372.2 0.6 copy.72
  372.8 1.5 fusion.6
  374.3 0.9 fusion.4
  375.2 0.0 copy-done.1
  (17 shorter events, 0.2 us)
Async XLA Ops:
  6.5 101.3 %copy-start = (s32[1024]{0:T(1024)S(1)}, s32[1024]{0:T(1024)}, u32[]{:S(2)}) copy-start(s32[1024]{0:T(1024)} %param.9) | copy-start | bytes 12292
  6.5 24.2 %copy-start.4 = (s32[8,16]{1,0:T(8,128)S(1)}, s32[8,16]{1,0:T(8,128)}, u32[]{:S(2)}) copy-start(s32[8,16]{1,0:T(8,128)} %param.7) | copy-start | bytes 1540
  9.0 14.4 %all-to-all-start = ((s32[8,1,2]{2,1,0:T(1,128)}), s32[8,1,2]{2,1,0:T(1,128)S(1)}, u32[]{:S(2)}, u32[]{:S(2)}) async-start(s32[8,1,2]{2,1,0:T(1,128)} %bitcast.46), calls=%async_computation | async-start | bytes 8192 | tf_op jit(solution)/shard_map/all_to_all | solution.py:40
  25.3 28.6 %all-to-all-start.1 = ((f32[8,2,128,128]{3,2,1,0:T(8,128)}), f32[8,2,128,128]{3,2,1,0:T(8,128)S(1)}, u32[]{:S(2)}, u32[]{:S(2)}) async-start(f32[8,2,128,128]{3,2,1,0:T(8,128)} %bitcast.2), calls=%async_computation.1 | async-start | bytes 2097152 | tf_op jit(solution)/shard_map/all_to_all | solution.py:48
  30.7 169.6 %reduce-scatter.2.cloned.1.call-start = ((), (), s32[]{:S(2)}) async-start(), calls=%async_computation.11 | async-start | bytes 10485760 | tf_op jit(solution)/shard_map/reduce_scatter | solution.py:59
  78.3 1.0 copy-start.3
  100.8 94.8 %all-to-all-start.3 = ((bf16[8,16,128,128]{3,2,1,0:T(8,128)(2,1)}), bf16[8,16,128,128]{3,2,1,0:T(8,128)(2,1)}, u32[]{:S(2)}, u32[]{:S(2)}) async-start(bf16[8,16,128,128]{3,2,1,0:T(8,128)(2,1)} %bitcast.96), calls=%async_computation.4 | async-start | bytes 8388608 | tf_op jit(solution)/shard_map/all_to_all | solution.py:85
  200.3 4.1 %copy-start.2 = (bf16[2,16,4,128,128]{4,3,2,1,0:T(8,128)(2,1)S(1)}, bf16[2,16,4,128,128]{4,3,2,1,0:T(8,128)(2,1)}, u32[]{:S(2)}) copy-start(bf16[2,16,4,128,128]{4,3,2,1,0:T(8,128)(2,1)} %copy.62) | copy-start | bytes 12582916
  372.2 3.0 copy-start.1
Sparse Core Ops, SparseCore 0:
  78.4 113.0 reduce-scatter.1
where the time goes:
time: 387 us; the launch traced here: 382 us
  blocking collectives  180 us (47%)
  waiting for transfers between devices  108 us (28%)
  local copies, waits for them, and re-layouts  36.1 us (9%)
  starting transfers between devices  18.1 us (5%)
  matrix products  15.5 us (4%)
  between operations  13.6 us (4%)
  other arithmetic  10.6 us (3%)
    all_to_all x2, blocking collectives, shards(): lax.all_to_all(near, 'dim', split_axis=0, concat_axis=2, tiled=True)  107 us
    all_to_all x1, waiting for transfers between devices, shards(): lax.all_to_all(near, 'dim', split_axis=0, concat_axis=2, tiled=True)  86.9 us
    all_to_all x3, blocking collectives, shards(): lax.all_to_all(sending, 'rows', split_axis=0, concat_axis=0, tiled=True)  50.5 us
    all_to_all x1, waiting for transfers between devices, shards(): lax.all_to_all(outgoing, 'rows', split_axis=0, concat_axis=0, tiled=True)  21.3 us
    all_to_all x2, blocking collectives, shards(): lax.all_to_all(fresh, 'dim', split_axis=1, concat_axis=0, tiled=True)  16.4 us
    gather x2, local copies, waits for them, and re-layouts, shards(): keys = arrived[flat]  13.4 us
    unnamed x1, matrix products  10.9 us
    gather x3, local copies, waits for them, and re-layouts, shards(): near = came[flat]  9.08 us
  transfers between devices with their start and end apart: 4, of which 2 were waited for; matrix products, arithmetic and copies ran while one was open for 4% of the time, Pallas kernels for 0%

commit v1 on v0

v1 whole, which is shorter than its diff:
```python
import jax
import jax.numpy as jnp
from jax import lax
from jax.sharding import PartitionSpec as P

ITERS = 3


sharpness = 16.0
seed_weight = 0.5
label_floor = 0.001
norm_eps = 1e-06


def shards(embeddings, prior, neighbours, seed_mask, families):
    groups = lax.axis_size("rows")
    splits = lax.axis_size("dim")
    member = lax.axis_index("dim")
    blocks = neighbours.shape[0]
    links = neighbours.shape[1]
    width = embeddings.shape[1]
    block_rows = embeddings.shape[2]
    fam_part = prior.shape[1]
    fam_all = fam_part * splits
    slots = blocks // 4
    owned = blocks // splits
    candidates = groups * slots
    shared = candidates == links
    places = jnp.arange(blocks, dtype=jnp.int32)
    everything = groups * blocks
    hits = neighbours[:, :, None] == jnp.arange(everything, dtype=jnp.int32)[None, None, :]
    named = jnp.any(hits, axis=(0, 1)).reshape(groups, blocks)
    upto = (places[None, :] <= places[:, None]).astype(jnp.int32)
    order = jnp.sum(named.astype(jnp.int32)[:, None, :] * upto[None, :, :], axis=2) - 1
    chosen = named[:, None, :] & (order[:, None, :] == jnp.arange(slots, dtype=jnp.int32)[None, :, None])
    ranked = jnp.sum(jnp.where(chosen, places[None, None, :], 0), axis=2)
    wanted = lax.all_to_all(ranked, "rows", split_axis=0, concat_axis=0, tiled=True)
    local_squares = jnp.sum(embeddings * embeddings, axis=1)
    raised_prior = jnp.exp(prior)
    local_total = jnp.sum(raised_prior, axis=1)
    squares, prior_total = lax.psum((local_squares, local_total), "dim")
    unit_blocks = (embeddings * lax.rsqrt(squares + norm_eps)[:, None, :]).astype(jnp.bfloat16)
    labels = (raised_prior / prior_total[:, None, :]).astype(jnp.bfloat16)
    both = jnp.concatenate([unit_blocks, labels], axis=1)
    queries = lax.all_gather(unit_blocks, "dim", axis=1, tiled=True)
    arrived = lax.all_to_all(both[wanted], "rows", split_axis=0, concat_axis=0, tiled=True).reshape(
        candidates, width + fam_part, block_rows
    )
    came = arrived[:, width:]
    keys = lax.all_gather(arrived[:, :width], "dim", axis=1, tiled=True)
    if shared:
        cosine = jnp.einsum("sek,qer->skqr", keys, queries, preferred_element_type=jnp.float32)
        raised = jnp.exp(sharpness * (cosine - 1.0))
        weights = (raised / jnp.sum(raised, axis=(0, 1), keepdims=True)).astype(jnp.bfloat16)
    else:
        owner = neighbours // blocks
        within = neighbours % blocks
        match = (within[:, :, None] == places[None, None, :]).astype(jnp.int32)
        flat = owner * slots + jnp.sum(match * order[owner], axis=2)

        def block_weights(packed):
            query, listed = packed
            cosine = jnp.einsum(
                "sek,er->skr", keys[listed], query, preferred_element_type=jnp.float32
            )
            raised = jnp.exp(sharpness * (cosine - 1.0))
            return (raised / jnp.sum(raised, axis=(0, 1), keepdims=True)).astype(jnp.bfloat16)

        weights = lax.map(block_weights, (queries, flat))
    hot = families.reshape(blocks, 1, block_rows) - member * fam_part
    seeds = jnp.where(
        hot == jnp.arange(fam_part, dtype=jnp.int32)[None, :, None],
        seed_weight * seed_mask.astype(jnp.float32).reshape(blocks, 1, block_rows),
        0.0,
    )
    shifted = seeds
    for sweep in range(ITERS):
        if sweep > 0:
            came = lax.all_to_all(
                labels[wanted], "rows", split_axis=0, concat_axis=0, tiled=True
            ).reshape(candidates, fam_part, block_rows)
        if shared:
            mixed = jnp.einsum("sfk,skqr->qfr", came, weights, preferred_element_type=jnp.float32)
        else:
            near = came

            def block_mix(packed):
                weight, listed = packed
                return jnp.einsum(
                    "sfk,skr->fr", near[listed], weight, preferred_element_type=jnp.float32
                )

            mixed = lax.map(block_mix, (weights, flat))
        shifted = mixed + seeds + label_floor
        if sweep + 1 < ITERS:
            squared = shifted * shifted
            total = lax.psum(jnp.sum(squared, axis=1), "dim")
            labels = (squared / total[:, None, :]).astype(jnp.bfloat16)
    mine = lax.all_to_all(shifted, "dim", split_axis=0, concat_axis=1, tiled=True)
    total = jnp.sum(mine * mine, axis=1, keepdims=True)
    result = 2.0 * jnp.log(mine) - jnp.log(total) + jnp.log(jnp.float32(fam_all))
    return jnp.transpose(result, (0, 2, 1)).reshape(owned * block_rows, fam_all)


def solution(mesh):
    return jax.shard_map(
        shards,
        mesh=mesh,
        in_specs=(
            P("rows", "dim", None),
            P("rows", "dim", None),
            P("rows", None),
            P("rows"),
            P("rows"),
        ),
        out_specs=P(("rows", "dim"), None),
        check_vma=False,
    )
```

time: 387 us -> 168 us (0.43)
  the two profiles are of different devices: /device:TPU:11 before, /device:TPU:0 now
where the time goes in v1:
time: 168 us; the launch traced here: 167 us
  blocking collectives  67.1 us (40%)
  waiting for transfers between devices  47.3 us (28%)
  between operations  13.6 us (8%)
  starting transfers between devices  12.7 us (8%)
  matrix products  11.3 us (7%)
  local copies, waits for them, and re-layouts  8.37 us (5%)
  other arithmetic  6.9 us (4%)
    all_to_all x2, blocking collectives, shards(): lax.all_to_all(labels[wanted], 'rows', split_axis=0, concat_axis=0, tiled...  37.2 us
    all_to_all x1, waiting for transfers between devices, shards(): lax.all_to_all(both[wanted], 'rows', split_axis=0, concat_axis=0, tiled=T...  24.8 us
    all_gather x1, waiting for transfers between devices, shards(): keys = lax.all_gather(arrived[:, :width], 'dim', axis=1, tiled=True)  21.8 us
    psum x2, blocking collectives, shards(): total = lax.psum(jnp.sum(squared, axis=1), 'dim')  11.9 us
    all_to_all x1, blocking collectives, shards(): lax.all_to_all(shifted, 'dim', split_axis=0, concat_axis=1, tiled=True)  11.2 us
    all_to_all x1, starting transfers between devices, shards(): lax.all_to_all(ranked, 'rows', split_axis=0, concat_axis=0, tiled=True)  7.25 us
    psum x1, blocking collectives, shards(): squares, prior_total = lax.psum((local_squares, local_total), 'dim')  6.74 us
    dot_general x3, matrix products, shards(): jnp.einsum('sfk,skqr->qfr', came, weights, preferred_element_type=jnp.flo...  6.71 us
  transfers between devices with their start and end apart: 4, of which 2 were waited for; matrix products, arithmetic and copies ran while one was open for 3% of the time, Pallas kernels for 0%

profile of v1, /device:TPU:0, one launch (start us, length us, event | category | flops | bytes accessed | tf_op | source)
XLA Modules:
  0.0 167.3 jit_solution(15970550586666391398)
XLA Ops:
  6.5 0.0 copy-start.2
  6.5 0.0 copy-start.3
  6.5 0.8 fusion.13
  7.4 0.1 and.11
  7.4 0.2 multiply_reduce_fusion.2
  7.7 0.1 select_reduce_fusion
  7.8 0.7 copy.46
  8.5 7.3 %all-to-all-start = ((s32[8,1,2]{2,1,0:T(1,128)}), s32[8,1,2]{2,1,0:T(1,128)S(1)}, u32[]{:S(2)}, u32[]{:S(2)}) async-start(s32[8,1,2]{2,1,0:T(1,128)} %copy.46), calls=%async_computation | async-start | bytes 8192 | tf_op jit(solution)/shard_map/all_to_all | solution.py:37
  15.8 1.3 multiply_reduce_fusion.1
  17.1 6.7 %all-reduce = (f32[8,128]{1,0:T(8,128)S(1)}, f32[8,128]{1,0:T(8,128)S(1)}) all-reduce(f32[8,128]{1,0:T(8,128)S(1)} %get-tuple-element.16, f32[8,128]{1,0:T(8,128)S(1)} %get-tuple-element.15), channel_id=1, replica_groups=mesh['rows'=8,'dim'=4] {'dim'}, use_global_device_ids=true, to_apply=%region_3.4 | all-reduce | flops 2048 | bytes 16384 | tf_op jit(solution)/shard_map/psum | solution.py:41
  23.8 1.1 multiply_convert_fusion
  24.9 0.0 copy-start.1
  24.9 1.2 divide_convert_fusion.3
  26.2 0.0 all-to-all-done
  26.2 0.1 copy.47
  26.3 0.1 copy.48
  26.4 0.1 reshape.109
  26.5 1.7 gather_fusion
  28.2 5.4 %all-to-all-start.1 = ((bf16[8,2,256,128]{3,2,1,0:T(8,128)(2,1)}), bf16[8,2,256,128]{3,2,1,0:T(8,128)(2,1)S(1)}, u32[]{:S(2)}, u32[]{:S(2)}) async-start(bf16[8,2,256,128]{3,2,1,0:T(8,128)(2,1)} %bitcast.2), calls=%async_computation.1 | async-start | bytes 2097152 | tf_op jit(solution)/shard_map/all_to_all | solution.py:46
  33.6 0.0 all-gather.5.cloned.1.call-start
  33.6 0.0 copy-done.1
  33.6 0.7 all-gather.5.cloned.1.call-update
  34.3 0.0 all-gather.3.cloned.1.call-start
  34.4 24.8 %all-to-all-done.1 = bf16[8,2,256,128]{3,2,1,0:T(8,128)(2,1)S(1)} async-done(((bf16[8,2,256,128]{3,2,1,0:T(8,128)(2,1)}), bf16[8,2,256,128]{3,2,1,0:T(8,128)(2,1)S(1)}, u32[]{:S(2)}, u32[]{:S(2)}) %all-to-all-start.1) | async-done | bytes 1048608 | tf_op jit(solution)/shard_map/all_to_all | solution.py:46
  59.1 0.5 copy.49
  59.7 0.9 slice.14
  60.6 0.0 all-gather.3.cloned.1.call-update
  60.6 0.0 copy-done.2
  60.6 0.0 copy-done.3
  60.6 0.0 all-gather.5.cloned.1.call-done
  60.7 21.8 %all-gather.3.cloned.1.call-done = bf16[16,512,128]{1,2,0:T(8,128)(2,1)} async-done(((bf16[16,128,128]{1,2,0:T(8,128)(2,1)}), bf16[16,512,128]{1,2,0:T(8,128)(2,1)}) %all-gather.3.cloned.1.call-update) | async-done | bytes 2097168 | tf_op jit(solution)/shard_map/all_gather | solution.py:50
  82.4 4.6 %fusion = (f32[8,128]{1,0:T(8,128)S(1)}, f32[16,128,8,128]{3,1,2,0:T(8,128)S(1)}) fusion(bf16[8,512,128]{2,1,0:T(8,128)(2,1)} %all-gather.5.cloned.1.call-done, bf16[16,512,128]{1,2,0:T(8,128)(2,1)} %all-gather.3.cloned.1.call-done), kind=kOutput, calls=%fused_computation.5 | convolution fusion | flops 2153774080 | bytes 11538432 | tf_op jit(solution)/shard_map/sek,qer->skqr/dot_general | solution.py:52
  87.0 1.8 %divide_convert_fusion = bf16[16,128,8,128]{3,1,2,0:T(8,128)(2,1)S(1)} fusion(f32[16,128,8,128]{3,1,2,0:T(8,128)S(1)} %get-tuple-element.10, f32[8,128]{1,0:T(8,128)S(1)} %get-tuple-element.9), kind=kLoop, calls=%fused_computation.3 | loop fusion | flops 8388608 | bytes 12587008 | tf_op jit(solution)/shard_map/convert_element_type | solution.py:54
  88.8 0.0 copy-start
  88.8 1.9 %copy-done = bf16[16,128,8,128]{3,1,2,0:T(8,128)(2,1)} copy-done((bf16[16,128,8,128]{3,1,2,0:T(8,128)(2,1)}, bf16[16,128,8,128]{3,1,2,0:T(8,128)(2,1)S(1)}, u32[]{:S(2)}) %copy-start) | copy-done | bytes 4194328
  90.7 0.8 fusion.16
  91.5 5.9 %psum.30 = f32[8,128]{1,0:T(8,128)S(1)} all-reduce(f32[8,128]{1,0:T(8,128)S(1)} %get-tuple-element.11), channel_id=1, replica_groups=mesh['rows'=8,'dim'=4] {'dim'}, use_global_device_ids=true, to_apply=%region_9.10 | all-reduce | flops 1024 | bytes 8192 | tf_op jit(solution)/shard_map/psum | solution.py:97
  97.4 0.1 divide_convert_fusion.2
  97.5 0.6 gather_fusion.1
  98.2 19.6 %all_to_all.36 = bf16[8,2,128,128]{3,2,1,0:T(8,128)(2,1)S(1)} all-to-all(bf16[8,2,128,128]{3,2,1,0:T(8,128)(2,1)S(1)} %bitcast.92), channel_id=1, replica_groups=mesh['rows'=8,'dim'=4] {'rows'}, dimensions={0} | all-to-all | bytes 1048576 | tf_op jit(solution)/shard_map/all_to_all | solution.py:79
  117.7 3.0 %fusion.17 = (f32[8,128]{1,0:T(8,128)S(1)}, f32[8,128,128]{2,1,0:T(8,128)S(1)}) fusion(f32[8,128]{1,0:T(8,128)S(1)} %multiply_bitcast_fusion, s32[8,128]{1,0:T(8,128)S(1)} %subtract_bitcast_fusion, bf16[16,128,128,1]{2,1,3,0:T(8,128)(2,1)S(1)} %bitcast.88, bf16[16,128,8,128]{3,1,2,0:T(8,128)(2,1)} %copy-done), kind=kOutput, calls=%fused_computation.48 | convolution fusion | flops 537656320 | bytes 5255168 | tf_op jit(solution)/shard_map/sfk,skqr->qfr/dot_general | solution.py:83
  120.7 6.0 %psum.31 = f32[8,128]{1,0:T(8,128)S(1)} all-reduce(f32[8,128]{1,0:T(8,128)S(1)} %get-tuple-element.13), channel_id=1, replica_groups=mesh['rows'=8,'dim'=4] {'dim'}, use_global_device_ids=true, to_apply=%region_11.12 | all-reduce | flops 1024 | bytes 8192 | tf_op jit(solution)/shard_map/psum | solution.py:97
  126.7 0.1 divide_convert_fusion.1
  126.7 0.6 gather_fusion.2
  127.4 17.7 %all_to_all.37 = bf16[8,2,128,128]{3,2,1,0:T(8,128)(2,1)S(1)} all-to-all(bf16[8,2,128,128]{3,2,1,0:T(8,128)(2,1)S(1)} %bitcast.91), channel_id=1, replica_groups=mesh['rows'=8,'dim'=4] {'rows'}, dimensions={0} | all-to-all | bytes 1048576 | tf_op jit(solution)/shard_map/all_to_all | solution.py:79
  145.0 2.9 %fusion.10 = f32[8,128,128]{2,1,0:T(8,128)S(1)} fusion(bf16[16,128,128,1]{2,1,3,0:T(8,128)(2,1)S(1)} %bitcast.87, bf16[16,128,8,128]{3,1,2,0:T(8,128)(2,1)} %copy-done, f32[8,128]{1,0:T(8,128)S(1)} %multiply_bitcast_fusion, s32[8,128]{1,0:T(8,128)S(1)} %subtract_bitcast_fusion), kind=kOutput, calls=%fused_computation.18 | convolution fusion | flops 537395200 | bytes 5251072 | tf_op jit(solution)/shard_map/sfk,skqr->qfr/dot_general | solution.py:83
  148.0 11.2 %all_to_all.38 = f32[8,128,128]{2,1,0:T(8,128)S(1)} all-to-all(f32[8,128,128]{2,1,0:T(8,128)S(1)} %fusion.10), channel_id=1, replica_groups=mesh['rows'=8,'dim'=4] {'dim'}, dimensions={0} | all-to-all | bytes 1048576 | tf_op jit(solution)/shard_map/all_to_all | solution.py:99
  159.2 0.1 multiply_reduce_fusion
  159.4 0.1 fusion.12
  159.5 1.0 copy.55
  (12 shorter events, 0.1 us)
Async XLA Ops:
  6.5 54.1 %copy-start.2 = (s32[1024]{0:T(1024)S(1)}, s32[1024]{0:T(1024)}, u32[]{:S(2)}) copy-start(s32[1024]{0:T(1024)} %param.8) | copy-start | bytes 12292
  6.5 54.1 %copy-start.3 = (s32[1024]{0:T(1024)S(1)}, s32[1024]{0:T(1024)}, u32[]{:S(2)}) copy-start(s32[1024]{0:T(1024)} %param.9) | copy-start | bytes 12292
  8.5 17.7 %all-to-all-start = ((s32[8,1,2]{2,1,0:T(1,128)}), s32[8,1,2]{2,1,0:T(1,128)S(1)}, u32[]{:S(2)}, u32[]{:S(2)}) async-start(s32[8,1,2]{2,1,0:T(1,128)} %copy.46), calls=%async_computation | async-start | bytes 8192 | tf_op jit(solution)/shard_map/all_to_all | solution.py:37
  24.9 8.7 %copy-start.1 = (bf16[8,128,128]{2,1,0:T(8,128)(2,1)}, bf16[8,128,128]{2,1,0:T(8,128)(2,1)S(1)}, u32[]{:S(2)}) copy-start(bf16[8,128,128]{2,1,0:T(8,128)(2,1)S(1)} %multiply_convert_fusion) | copy-start | bytes 786436
  28.2 31.0 %all-to-all-start.1 = ((bf16[8,2,256,128]{3,2,1,0:T(8,128)(2,1)}), bf16[8,2,256,128]{3,2,1,0:T(8,128)(2,1)S(1)}, u32[]{:S(2)}, u32[]{:S(2)}) async-start(bf16[8,2,256,128]{3,2,1,0:T(8,128)(2,1)} %bitcast.2), calls=%async_computation.1 | async-start | bytes 2097152 | tf_op jit(solution)/shard_map/all_to_all | solution.py:46
  33.6 27.1 %all-gather.5.cloned.1.call-start = ((), (), s32[]{:S(2)}) async-start(), calls=%async_computation.6 | async-start | bytes 1310720 | tf_op jit(solution)/shard_map/all_gather | solution.py:45
  34.3 48.1 %all-gather.3.cloned.1.call-start = ((), (), s32[]{:S(2)}) async-start(), calls=%async_computation.5 | async-start | bytes 2621440 | tf_op jit(solution)/shard_map/all_gather | solution.py:50
  88.8 1.9 %copy-start = (bf16[16,128,8,128]{3,1,2,0:T(8,128)(2,1)}, bf16[16,128,8,128]{3,1,2,0:T(8,128)(2,1)S(1)}, u32[]{:S(2)}) copy-start(bf16[16,128,8,128]{3,1,2,0:T(8,128)(2,1)S(1)} %divide_convert_fusion) | copy-start | bytes 12582916
Sparse Core Ops, SparseCore 0:
  36.0 17.9 all-gather.4
  60.7 21.6 all-gather.2

commit v2 on v1

v2 whole, which is shorter than its diff:
```python
import functools

import jax
import jax.numpy as jnp
from jax import lax
from jax.experimental import pallas as pl
from jax.experimental.pallas import tpu as pltpu
from jax.sharding import PartitionSpec as P

ITERS = 3


sharpness = 16.0
seed_weight = 0.5
label_floor = 0.001
norm_eps = 1e-06


def propagate(
    groups, splits, slots,
    wanted, unit, wide, labels, seeds, out,
    q_all, k_all, w_all, near, stage_u, stage_l, mixed, fresh, tot_mine, tot_got, fin_out,
    send_u, recv_u, send_l, recv_l, send_q, recv_q, send_k, recv_k, send_t, recv_t, send_f, recv_f,
):
    me = lax.axis_index("rows")
    member = lax.axis_index("dim")
    blocks, width, block_rows = unit.shape
    fam = labels.shape[1]
    rows = blocks * block_rows
    pair = slots * block_rows
    own = rows // splits
    bar = pltpu.get_barrier_semaphore()

    def row_peer(k):
        return {"rows": lax.rem(me + k, groups)}

    def dim_peer(j):
        return {"dim": lax.rem(member + j, splits)}

    def remote(src, dst, send, recv, peer):
        return pltpu.make_async_remote_copy(
            src_ref=src, dst_ref=dst, send_sem=send, recv_sem=recv,
            device_id=peer, device_id_type=pl.DeviceIdType.MESH,
        )

    def unit_copy(k):
        return remote(
            stage_u.at[k], k_all.at[k, pl.ds(0, width), :], send_u.at[k], recv_u.at[k], row_peer(k)
        )

    def label_copy(t, k):
        return remote(
            stage_l.at[t, k], near.at[t, k], send_l.at[t, k], recv_l.at[t, k], row_peer(k)
        )

    def query_copy(j):
        return remote(
            q_all.at[pl.ds(0, width), :], q_all.at[pl.ds(j * width, width), :],
            send_q.at[j], recv_q.at[j], dim_peer(j),
        )

    def key_copy(k, j):
        return remote(
            k_all.at[k, pl.ds(0, width), :], k_all.at[k, pl.ds(j * width, width), :],
            send_k.at[k, j], recv_k.at[k, j], dim_peer(j),
        )

    def total_copy(t, j):
        return remote(
            tot_mine.at[t], tot_got.at[t, j], send_t.at[t, j], recv_t.at[t, j], dim_peer(j)
        )

    def final_copy(j):
        return remote(
            fin_out.at[lax.rem(member + j, splits)], out.at[member], send_f.at[j], recv_f.at[j],
            dim_peer(j),
        )

    for k in range(1, groups):
        pl.semaphore_signal(bar, inc=1, device_id=row_peer(k), device_id_type=pl.DeviceIdType.MESH)
    for j in range(1, splits):
        pl.semaphore_signal(bar, inc=1, device_id=dim_peer(j), device_id_type=pl.DeviceIdType.MESH)

    q_all[0:width, :] = wide[...]

    def pick(k, s):
        return wanted[lax.rem(me + k, groups), s]

    for s in range(slots):
        k_all[0, 0:width, s * block_rows:(s + 1) * block_rows] = unit[pick(0, s)]
        near[0, 0, :, s * block_rows:(s + 1) * block_rows] = labels[pick(0, s)]
    pl.semaphore_wait(bar, groups + splits - 2)

    @pl.loop(1, groups)
    def _(k):
        for s in range(slots):
            stage_u[k, :, s * block_rows:(s + 1) * block_rows] = unit[pick(k, s)]
        unit_copy(k).start()

    for j in range(1, splits):
        query_copy(j).start()
    for j in range(1, splits):
        key_copy(0, j).start()

    @pl.loop(1, groups)
    def _(k):
        for s in range(slots):
            stage_l[0, k, :, s * block_rows:(s + 1) * block_rows] = labels[pick(k, s)]
        label_copy(0, k).start()

    for j in range(1, splits):
        query_copy(j).wait_recv()
    tot_mine[ITERS - 1] = jnp.zeros((1, rows), jnp.float32)

    def score(k):
        for j in range(1, splits):
            key_copy(k, j).wait_recv()

        @pl.loop(0, splits)
        def _(c):
            cols = pl.ds(pl.multiple_of(c * own, own), own)
            cosine = lax.dot_general(
                k_all[k], q_all[:, cols], (((0,), (0,)), ((), ())),
                preferred_element_type=jnp.float32,
            )
            raised = jnp.exp(sharpness * (cosine - 1.0))
            w_all[k, :, cols] = raised.astype(jnp.bfloat16)
            tot_mine[ITERS - 1, :, cols] += jnp.sum(raised, axis=0, keepdims=True)

    @pl.loop(1, groups)
    def _(k):
        unit_copy(k).wait_recv()
        for j in range(1, splits):
            key_copy(k, j).start()
        score(k - 1)

    score(groups - 1)

    for t in range(ITERS):
        mixed[...] = jnp.dot(near[t, 0], w_all[0], preferred_element_type=jnp.float32)

        @pl.loop(1, groups)
        def _(k):
            label_copy(t, k).wait_recv()
            mixed[...] += jnp.dot(near[t, k], w_all[k], preferred_element_type=jnp.float32)

        shifted = mixed[...] / tot_mine[ITERS - 1] + seeds[...] + label_floor
        if t + 1 < ITERS:
            squared = shifted * shifted
            mixed[...] = squared
            tot_mine[t] = jnp.sum(squared, axis=0, keepdims=True)
            for j in range(1, splits):
                total_copy(t, j).start()
            for j in range(1, splits):
                total_copy(t, j).wait_recv()
            total = tot_mine[t]
            for j in range(1, splits):
                total = total + tot_got[t, j]
            soft = (mixed[...] / total).astype(jnp.bfloat16)
            for b in range(blocks):
                fresh[t, b] = soft[:, b * block_rows:(b + 1) * block_rows]

            @pl.loop(1, groups)
            def _(k):
                for s in range(slots):
                    stage_l[t + 1, k, :, s * block_rows:(s + 1) * block_rows] = fresh[t, pick(k, s)]
                label_copy(t + 1, k).start()

            for s in range(slots):
                near[t + 1, 0, :, s * block_rows:(s + 1) * block_rows] = fresh[t, pick(0, s)]
        else:
            for m in range(splits):
                fin_out[m] = shifted[:, m * own:(m + 1) * own]
            for j in range(1, splits):
                final_copy(j).start()
            out[member] = fin_out[member]

    for j in range(1, splits):
        final_copy(j).wait_recv()
        final_copy(j).wait_send()
        query_copy(j).wait_send()
        key_copy(0, j).wait_send()
        for t in range(ITERS - 1):
            total_copy(t, j).wait_send()

    @pl.loop(1, groups)
    def _(k):
        unit_copy(k).wait_send()
        for j in range(1, splits):
            key_copy(k, j).wait_send()
        for t in range(ITERS):
            label_copy(t, k).wait_send()


def fused(groups, splits, slots, wanted, unit, wide, labels, seeds):
    blocks, width, block_rows = unit.shape
    fam = labels.shape[1]
    rows = blocks * block_rows
    pair = slots * block_rows
    own = rows // splits
    vmem = pl.BlockSpec(memory_space=pltpu.VMEM)
    dma = pltpu.SemaphoreType.DMA
    return pl.pallas_call(
        functools.partial(propagate, groups, splits, slots),
        out_shape=jax.ShapeDtypeStruct((splits, fam, own), jnp.float32),
        in_specs=[pl.BlockSpec(memory_space=pltpu.SMEM)] + [vmem] * 4,
        out_specs=vmem,
        scratch_shapes=[
            pltpu.VMEM((splits * width, rows), jnp.bfloat16),
            pltpu.VMEM((groups, splits * width, pair), jnp.bfloat16),
            pltpu.VMEM((groups, pair, rows), jnp.bfloat16),
            pltpu.VMEM((ITERS, groups, fam, pair), jnp.bfloat16),
            pltpu.VMEM((groups, width, pair), jnp.bfloat16),
            pltpu.VMEM((ITERS, groups, fam, pair), jnp.bfloat16),
            pltpu.VMEM((fam, rows), jnp.float32),
            pltpu.VMEM((ITERS - 1, blocks, fam, block_rows), jnp.bfloat16),
            pltpu.VMEM((ITERS, 1, rows), jnp.float32),
            pltpu.VMEM((ITERS - 1, splits, 1, rows), jnp.float32),
            pltpu.VMEM((splits, fam, own), jnp.float32),
            dma((groups,)), dma((groups,)),
            dma((ITERS, groups)), dma((ITERS, groups)),
            dma((splits,)), dma((splits,)),
            dma((groups, splits)), dma((groups, splits)),
            dma((ITERS - 1, splits)), dma((ITERS - 1, splits)),
            dma((splits,)), dma((splits,)),
        ],
        compiler_params=pltpu.CompilerParams(
            collective_id=0, has_side_effects=True, vmem_limit_bytes=40 * 1024 * 1024
        ),
    )(wanted, unit, wide, labels, seeds)


def finish(mine, fam_all):
    total = jnp.sum(mine * mine, axis=-2, keepdims=True)
    return 2.0 * jnp.log(mine) - jnp.log(total) + jnp.log(jnp.float32(fam_all))


def shards(embeddings, prior, neighbours, seed_mask, families):
    groups = lax.axis_size("rows")
    splits = lax.axis_size("dim")
    member = lax.axis_index("dim")
    blocks = neighbours.shape[0]
    links = neighbours.shape[1]
    width = embeddings.shape[1]
    block_rows = embeddings.shape[2]
    fam_part = prior.shape[1]
    fam_all = fam_part * splits
    slots = blocks // 4
    owned = blocks // splits
    candidates = groups * slots
    shared = candidates == links
    places = jnp.arange(blocks, dtype=jnp.int32)
    everything = groups * blocks
    hits = neighbours[:, :, None] == jnp.arange(everything, dtype=jnp.int32)[None, None, :]
    named = jnp.any(hits, axis=(0, 1)).reshape(groups, blocks)
    upto = (places[None, :] <= places[:, None]).astype(jnp.int32)
    order = jnp.sum(named.astype(jnp.int32)[:, None, :] * upto[None, :, :], axis=2) - 1
    chosen = named[:, None, :] & (order[:, None, :] == jnp.arange(slots, dtype=jnp.int32)[None, :, None])
    ranked = jnp.sum(jnp.where(chosen, places[None, None, :], 0), axis=2)
    wanted = lax.all_to_all(ranked, "rows", split_axis=0, concat_axis=0, tiled=True)
    local_squares = jnp.sum(embeddings * embeddings, axis=1)
    raised_prior = jnp.exp(prior)
    local_total = jnp.sum(raised_prior, axis=1)
    squares, prior_total = lax.psum((local_squares, local_total), "dim")
    unit_blocks = (embeddings * lax.rsqrt(squares + norm_eps)[:, None, :]).astype(jnp.bfloat16)
    labels = (raised_prior / prior_total[:, None, :]).astype(jnp.bfloat16)
    hot = families.reshape(blocks, 1, block_rows) - member * fam_part
    seeds = jnp.where(
        hot == jnp.arange(fam_part, dtype=jnp.int32)[None, :, None],
        seed_weight * seed_mask.astype(jnp.float32).reshape(blocks, 1, block_rows),
        0.0,
    )
    if shared:
        wide = jnp.transpose(unit_blocks, (1, 0, 2)).reshape(width, blocks * block_rows)
        seeds = jnp.transpose(seeds, (1, 0, 2)).reshape(fam_part, blocks * block_rows)
        mine = fused(groups, splits, slots, wanted, unit_blocks, wide, labels, seeds)
        return jnp.transpose(finish(mine.reshape(fam_all, owned * block_rows), fam_all))
    both = jnp.concatenate([unit_blocks, labels], axis=1)
    queries = lax.all_gather(unit_blocks, "dim", axis=1, tiled=True)
    arrived = lax.all_to_all(both[wanted], "rows", split_axis=0, concat_axis=0, tiled=True).reshape(
        candidates, width + fam_part, block_rows
    )
    came = arrived[:, width:]
    keys = lax.all_gather(arrived[:, :width], "dim", axis=1, tiled=True)
    owner = neighbours // blocks
    within = neighbours % blocks
    match = (within[:, :, None] == places[None, None, :]).astype(jnp.int32)
    flat = owner * slots + jnp.sum(match * order[owner], axis=2)

    def block_weights(packed):
        query, listed = packed
        cosine = jnp.einsum(
            "sek,er->skr", keys[listed], query, preferred_element_type=jnp.float32
        )
        raised = jnp.exp(sharpness * (cosine - 1.0))
        return (raised / jnp.sum(raised, axis=(0, 1), keepdims=True)).astype(jnp.bfloat16)

    weights = lax.map(block_weights, (queries, flat))
    shifted = seeds
    for sweep in range(ITERS):
        if sweep > 0:
            came = lax.all_to_all(
                labels[wanted], "rows", split_axis=0, concat_axis=0, tiled=True
            ).reshape(candidates, fam_part, block_rows)
        near = came

        def block_mix(packed):
            weight, listed = packed
            return jnp.einsum(
                "sfk,skr->fr", near[listed], weight, preferred_element_type=jnp.float32
            )

        mixed = lax.map(block_mix, (weights, flat))
        shifted = mixed + seeds + label_floor
        if sweep + 1 < ITERS:
            squared = shifted * shifted
            total = lax.psum(jnp.sum(squared, axis=1), "dim")
            labels = (squared / total[:, None, :]).astype(jnp.bfloat16)
    mine = lax.all_to_all(shifted, "dim", split_axis=0, concat_axis=1, tiled=True)
    result = finish(mine, fam_all)
    return jnp.transpose(result, (0, 2, 1)).reshape(owned * block_rows, fam_all)


def solution(mesh):
    return jax.shard_map(
        shards,
        mesh=mesh,
        in_specs=(
            P("rows", "dim", None),
            P("rows", "dim", None),
            P("rows", None),
            P("rows"),
            P("rows"),
        ),
        out_specs=P(("rows", "dim"), None),
        check_vma=False,
    )
```

time: 168 us -> 102 us (0.61)
  the two profiles are of different devices: /device:TPU:0 before, /device:TPU:27 now
where the time goes in v2:
time: 102 us; the launch traced here: 101 us
  Pallas kernels  83.2 us (82%)
  blocking collectives  6.32 us (6%)
  starting transfers between devices  5.44 us (5%)
  local copies, waits for them, and re-layouts  3.25 us (3%)
  other arithmetic  3.09 us (3%)
    pallas_call x1, Pallas kernels, fused(): pl.pallas_call(functools.partial(propagate, groups, splits, slots), out_s...  83.2 us
    psum x1, blocking collectives, shards(): squares, prior_total = lax.psum((local_squares, local_total), 'dim')  6.32 us
    all_to_all x1, starting transfers between devices, shards(): lax.all_to_all(ranked, 'rows', split_axis=0, concat_axis=0, tiled=True)  5.44 us
    unnamed x10, local copies, waits for them, and re-layouts  2.27 us
  transfers between devices with their start and end apart: 1, of which 0 were waited for; matrix products, arithmetic and copies ran while one was open for 2% of the time, Pallas kernels for 0%

profile of v2, /device:TPU:27, one launch (start us, length us, event | category | flops | bytes accessed | tf_op | source)
XLA Modules:
  0.0 101.4 jit_solution(1781332057448689821)
XLA Ops:
  0.0 0.0 copy-start.2
  0.0 0.7 copy-done.2
  0.7 0.1 fusion.1
  0.8 0.1 and.11
  0.9 0.2 multiply_reduce_fusion.2
  1.1 0.1 select_reduce_fusion
  1.3 0.7 copy.14
  2.0 5.4 %all-to-all-start = ((s32[8,1,2]{2,1,0:T(1,128)}), s32[8,1,2]{2,1,0:T(1,128)S(1)}, u32[]{:S(2)}, u32[]{:S(2)}) async-start(s32[8,1,2]{2,1,0:T(1,128)} %copy.14), calls=%async_computation | async-start | bytes 8192 | tf_op jit(solution)/shard_map/all_to_all | solution.py:260
  7.4 0.0 copy-start
  7.4 1.4 %multiply_reduce_fusion.1 = (f32[8,128]{1,0:T(8,128)S(1)}, f32[8,128]{1,0:T(8,128)S(1)}) fusion(f32[8,128,128]{2,1,0:T(8,128)} %param.5, f32[8,128,128]{2,1,0:T(8,128)} %param.6), kind=kLoop, calls=%fused_computation.6 | loop fusion | flops 391168 | bytes 1056768 | tf_op jit(solution)/shard_map/reduce_sum | solution.py:261
  8.8 6.3 %all-reduce = (f32[8,128]{1,0:T(8,128)S(1)}, f32[8,128]{1,0:T(8,128)S(1)}) all-reduce(f32[8,128]{1,0:T(8,128)S(1)} %get-tuple-element.9, f32[8,128]{1,0:T(8,128)S(1)} %get-tuple-element.10), channel_id=1, replica_groups=mesh['rows'=8,'dim'=4] {'dim'}, use_global_device_ids=true, to_apply=%region_4.5 | all-reduce | flops 2048 | bytes 16384 | tf_op jit(solution)/shard_map/psum | solution.py:264
  15.1 0.0 copy-done
  15.2 0.0 copy-start.3
  15.2 0.0 copy-start.1
  15.2 0.6 copy-done.3
  15.8 0.4 copy-done.1
  16.2 0.0 copy-start.4
  16.2 0.1 divide_convert_fusion.labels
  16.3 0.6 copy-done.4
  16.9 0.1 fusion.seeds
  17.0 0.0 all-to-all-done
  17.0 83.2 %shard_map.55 = f32[4,128,256]{2,1,0:T(8,128)S(1)} custom-call(s32[8,2]{1,0:T(8,128)S(1)} %bitcast.11, bf16[8,128,128]{2,1,0:T(8,128)(2,1)S(1)} %multiply_convert_fusion.unit, bf16[128,1024]{1,0:T(8,128)(2,1)S(1)} %copy_bitcast_fusion.wide, bf16[8,128,128]{2,1,0:T(8,128)(2,1)S(1)} %divide_convert_fusion.labels, f32[128,1024]{1,0:T(8,128)S(1)} %fusion.seeds), custom_call_target="tpu_custom_call" | custom-call | tf_op jit(solution)/shard_map/pallas_call | solution.py:203
  100.2 0.1 multiply_reduce_fusion
  100.3 0.2 copy.18
  100.5 0.9 add_bitcast_fusion
  (9 shorter events, 0.1 us)
Async XLA Ops:
  0.0 0.7 copy-start.2
  2.0 15.0 %all-to-all-start = ((s32[8,1,2]{2,1,0:T(1,128)}), s32[8,1,2]{2,1,0:T(1,128)S(1)}, u32[]{:S(2)}, u32[]{:S(2)}) async-start(s32[8,1,2]{2,1,0:T(1,128)} %copy.14), calls=%async_computation | async-start | bytes 8192 | tf_op jit(solution)/shard_map/all_to_all | solution.py:260
  7.4 7.7 %copy-start = (f32[8,128,128]{2,1,0:T(8,128)S(1)}, f32[8,128,128]{2,1,0:T(8,128)}, u32[]{:S(2)}) copy-start(f32[8,128,128]{2,1,0:T(8,128)} %param.5) | copy-start | bytes 1572868
  15.2 0.7 copy-start.3
  15.2 1.0 %copy-start.1 = (f32[8,128,128]{2,1,0:T(8,128)S(1)}, f32[8,128,128]{2,1,0:T(8,128)}, u32[]{:S(2)}) copy-start(f32[8,128,128]{2,1,0:T(8,128)} %param.6) | copy-start | bytes 1572868
  16.2 0.7 copy-start.4

commit v3 on v2

--- a/solution.py
+++ b/solution.py
@@ -19,7 +19,7 @@
 def propagate(
     groups, splits, slots,
     wanted, unit, wide, labels, seeds, out,
-    q_all, k_all, w_all, near, stage_u, stage_l, mixed, fresh, tot_mine, tot_got, fin_out,
+    q_all, k_all, raw, w_all, near, stage_u, stage_l, mixed, fresh, tot_mine, tot_got, fin_out,
     send_u, recv_u, send_l, recv_l, send_q, recv_q, send_k, recv_k, send_t, recv_t, send_f, recv_f,
 ):
     me = lax.axis_index("rows")
@@ -34,8 +34,11 @@
     def row_peer(k):
         return {"rows": lax.rem(me + k, groups)}
 
+    mate = member + 1 - 2 * lax.rem(member, 2)
+    others = (member, mate, lax.rem(member + 2, splits), lax.rem(mate + 2, splits))
+
     def dim_peer(j):
-        return {"dim": lax.rem(member + j, splits)}
+        return {"dim": others[j]}
 
     def remote(src, dst, send, recv, peer):
         return pltpu.make_async_remote_copy(
@@ -55,14 +58,15 @@
 
     def query_copy(j):
         return remote(
-            q_all.at[pl.ds(0, width), :], q_all.at[pl.ds(j * width, width), :],
-            send_q.at[j], recv_q.at[j], dim_peer(j),
+            q_all.at[pl.ds((j // 3) * 2 * width, width), :], q_all.at[pl.ds(j * width, width), :],
+            send_q.at[j], recv_q.at[j], dim_peer(2 if j == 2 else 1),
         )
 
     def key_copy(k, j):
         return remote(
-            k_all.at[k, pl.ds(0, width), :], k_all.at[k, pl.ds(j * width, width), :],
-            send_k.at[k, j], recv_k.at[k, j], dim_peer(j),
+            k_all.at[k, pl.ds((j // 3) * 2 * width, width), :],
+            k_all.at[k, pl.ds(j * width, width), :],
+            send_k.at[k, j], recv_k.at[k, j], dim_peer(2 if j == 2 else 1),
         )
 
     def total_copy(t, j):
@@ -72,7 +76,7 @@
 
     def final_copy(j):
         return remote(
-            fin_out.at[lax.rem(member + j, splits)], out.at[member], send_f.at[j], recv_f.at[j],
+            fin_out.at[others[j]], out.at[member], send_f.at[j], recv_f.at[j],
             dim_peer(j),
         )
 
@@ -97,9 +101,9 @@
             stage_u[k, :, s * block_rows:(s + 1) * block_rows] = unit[pick(k, s)]
         unit_copy(k).start()
 
-    for j in range(1, splits):
+    for j in (2, 1):
         query_copy(j).start()
-    for j in range(1, splits):
+    for j in (2, 1):
         key_copy(0, j).start()
 
     @pl.loop(1, groups)
@@ -108,13 +112,15 @@
             stage_l[0, k, :, s * block_rows:(s + 1) * block_rows] = labels[pick(k, s)]
         label_copy(0, k).start()
 
-    for j in range(1, splits):
-        query_copy(j).wait_recv()
+    query_copy(2).wait_recv()
+    query_copy(3).start()
+    query_copy(1).wait_recv()
+    query_copy(3).wait_recv()
     tot_mine[ITERS - 1] = jnp.zeros((1, rows), jnp.float32)
 
     def score(k):
-        for j in range(1, splits):
-            key_copy(k, j).wait_recv()
+        key_copy(k, 1).wait_recv()
+        key_copy(k, 3).wait_recv()
 
         @pl.loop(0, splits)
         def _(c):
@@ -124,17 +130,35 @@
                 preferred_element_type=jnp.float32,
             )
             raised = jnp.exp(sharpness * (cosine - 1.0))
-            w_all[k, :, cols] = raised.astype(jnp.bfloat16)
+            raw[k, :, cols] = raised
             tot_mine[ITERS - 1, :, cols] += jnp.sum(raised, axis=0, keepdims=True)
 
-    @pl.loop(1, groups)
-    def _(k):
+    def spread(k):
         unit_copy(k).wait_recv()
-        for j in range(1, splits):
-            key_copy(k, j).start()
-        score(k - 1)
-
+        key_copy(k, 2).start()
+        key_copy(k, 1).start()
+
+    def hand_on(k):
+        key_copy(k, 2).wait_recv()
+        key_copy(k, 3).start()
+
+    spread(1)
+    hand_on(0)
+
+    @pl.loop(2, groups)
+    def _(k):
+        spread(k)
+        hand_on(k - 1)
+        score(k - 2)
+
+    hand_on(groups - 1)
+    score(groups - 2)
     score(groups - 1)
+    tot_mine[ITERS - 1] = 1.0 / tot_mine[ITERS - 1]
+
+    @pl.loop(0, groups)
+    def _(k):
+        w_all[k] = (raw[k] * tot_mine[ITERS - 1]).astype(jnp.bfloat16)
 
     for t in range(ITERS):
         mixed[...] = jnp.dot(near[t, 0], w_all[0], preferred_element_type=jnp.float32)
@@ -144,7 +168,7 @@
             label_copy(t, k).wait_recv()
             mixed[...] += jnp.dot(near[t, k], w_all[k], preferred_element_type=jnp.float32)
 
-        shifted = mixed[...] / tot_mine[ITERS - 1] + seeds[...] + label_floor
+        shifted = mixed[...] + seeds[...] + label_floor
         if t + 1 < ITERS:
             squared = shifted * shifted
             mixed[...] = squared
@@ -208,6 +232,7 @@
         scratch_shapes=[
             pltpu.VMEM((splits * width, rows), jnp.bfloat16),
             pltpu.VMEM((groups, splits * width, pair), jnp.bfloat16),
+            pltpu.VMEM((groups, pair, rows), jnp.float32),
             pltpu.VMEM((groups, pair, rows), jnp.bfloat16),
             pltpu.VMEM((ITERS, groups, fam, pair), jnp.bfloat16),
             pltpu.VMEM((groups, width, pair), jnp.bfloat16),
@@ -248,7 +273,7 @@
     slots = blocks // 4
     owned = blocks // splits
     candidates = groups * slots
-    shared = candidates == links
+    shared = candidates == links and splits == 4
     places = jnp.arange(blocks, dtype=jnp.int32)
     everything = groups * blocks
     hits = neighbours[:, :, None] == jnp.arange(everything, dtype=jnp.int32)[None, None, :]

time: 102 us -> 95.6 us (0.937)
  the two profiles are of different devices: /device:TPU:27 before, /device:TPU:11 now
where the time goes in v3:
time: 95.6 us; the launch traced here: 95.3 us
  Pallas kernels  76.8 us (80%)
  blocking collectives  6.32 us (7%)
  starting transfers between devices  5.66 us (6%)
  local copies, waits for them, and re-layouts  3.25 us (3%)
  other arithmetic  3.09 us (3%)
    pallas_call x1, Pallas kernels, fused(): pl.pallas_call(functools.partial(propagate, groups, splits, slots), out_s...  76.8 us
    psum x1, blocking collectives, shards(): squares, prior_total = lax.psum((local_squares, local_total), 'dim')  6.32 us
    all_to_all x1, starting transfers between devices, shards(): lax.all_to_all(ranked, 'rows', split_axis=0, concat_axis=0, tiled=True)  5.66 us
    unnamed x10, local copies, waits for them, and re-layouts  2.27 us
  transfers between devices with their start and end apart: 1, of which 0 were waited for; matrix products, arithmetic and copies ran while one was open for 2% of the time, Pallas kernels for 0%

profile of v3, /device:TPU:11, one launch (start us, length us, event | category | flops | bytes accessed | tf_op | source)
XLA Modules:
  0.0 95.3 jit_solution(14358981511612002172)
XLA Ops:
  0.0 0.0 copy-start.2
  0.0 0.7 copy-done.2
  0.7 0.1 fusion.1
  0.8 0.1 and.11
  0.9 0.2 multiply_reduce_fusion.2
  1.1 0.1 select_reduce_fusion
  1.3 0.7 copy.14
  2.0 5.7 %all-to-all-start = ((s32[8,1,2]{2,1,0:T(1,128)}), s32[8,1,2]{2,1,0:T(1,128)S(1)}, u32[]{:S(2)}, u32[]{:S(2)}) async-start(s32[8,1,2]{2,1,0:T(1,128)} %copy.14), calls=%async_computation | async-start | bytes 8192 | tf_op jit(solution)/shard_map/all_to_all | solution.py:285
  7.6 0.0 copy-start
  7.6 1.4 %multiply_reduce_fusion.1 = (f32[8,128]{1,0:T(8,128)S(1)}, f32[8,128]{1,0:T(8,128)S(1)}) fusion(f32[8,128,128]{2,1,0:T(8,128)} %param.5, f32[8,128,128]{2,1,0:T(8,128)} %param.6), kind=kLoop, calls=%fused_computation.6 | loop fusion | flops 391168 | bytes 1056768 | tf_op jit(solution)/shard_map/reduce_sum | solution.py:286
  9.0 6.3 %all-reduce = (f32[8,128]{1,0:T(8,128)S(1)}, f32[8,128]{1,0:T(8,128)S(1)}) all-reduce(f32[8,128]{1,0:T(8,128)S(1)} %get-tuple-element.9, f32[8,128]{1,0:T(8,128)S(1)} %get-tuple-element.10), channel_id=1, replica_groups=mesh['rows'=8,'dim'=4] {'dim'}, use_global_device_ids=true, to_apply=%region_4.5 | all-reduce | flops 2048 | bytes 16384 | tf_op jit(solution)/shard_map/psum | solution.py:289
  15.3 0.0 copy-done
  15.4 0.0 copy-start.3
  15.4 0.0 copy-start.1
  15.5 0.6 copy-done.3
  16.1 0.4 copy-done.1
  16.4 0.0 copy-start.4
  16.4 0.1 divide_convert_fusion.labels
  16.5 0.6 copy-done.4
  17.1 0.1 fusion.seeds
  17.2 0.0 all-to-all-done
  17.2 76.8 %shard_map.55 = f32[4,128,256]{2,1,0:T(8,128)S(1)} custom-call(s32[8,2]{1,0:T(8,128)S(1)} %bitcast.11, bf16[8,128,128]{2,1,0:T(8,128)(2,1)S(1)} %multiply_convert_fusion.unit, bf16[128,1024]{1,0:T(8,128)(2,1)S(1)} %copy_bitcast_fusion.wide, bf16[8,128,128]{2,1,0:T(8,128)(2,1)S(1)} %divide_convert_fusion.labels, f32[128,1024]{1,0:T(8,128)S(1)} %fusion.seeds), custom_call_target="tpu_custom_call" | custom-call | tf_op jit(solution)/shard_map/pallas_call | solution.py:227
  94.0 0.1 multiply_reduce_fusion
  94.2 0.2 copy.18
  94.4 0.9 add_bitcast_fusion
  (9 shorter events, 0.1 us)
Async XLA Ops:
  0.0 0.7 copy-start.2
  2.0 15.2 %all-to-all-start = ((s32[8,1,2]{2,1,0:T(1,128)}), s32[8,1,2]{2,1,0:T(1,128)S(1)}, u32[]{:S(2)}, u32[]{:S(2)}) async-start(s32[8,1,2]{2,1,0:T(1,128)} %copy.14), calls=%async_computation | async-start | bytes 8192 | tf_op jit(solution)/shard_map/all_to_all | solution.py:285
  7.6 7.7 %copy-start = (f32[8,128,128]{2,1,0:T(8,128)S(1)}, f32[8,128,128]{2,1,0:T(8,128)}, u32[]{:S(2)}) copy-start(f32[8,128,128]{2,1,0:T(8,128)} %param.5) | copy-start | bytes 1572868
  15.4 0.7 copy-start.3
  15.4 1.0 %copy-start.1 = (f32[8,128,128]{2,1,0:T(8,128)S(1)}, f32[8,128,128]{2,1,0:T(8,128)}, u32[]{:S(2)}) copy-start(f32[8,128,128]{2,1,0:T(8,128)} %param.6) | copy-start | bytes 1572868
  16.4 0.7 copy-start.4

commit v4 on v3

--- a/solution.py
+++ b/solution.py
@@ -18,16 +18,16 @@
 
 def propagate(
     groups, splits, slots,
-    wanted, unit, wide, labels, seeds, out,
+    ranks, emb, prior, seeds, out,
+    unit, labels, pre_mine, pre_got, rank_got, wanted,
     q_all, k_all, raw, w_all, near, stage_u, stage_l, mixed, fresh, tot_mine, tot_got, fin_out,
     send_u, recv_u, send_l, recv_l, send_q, recv_q, send_k, recv_k, send_t, recv_t, send_f, recv_f,
+    send_p, recv_p, send_r, recv_r, move,
 ):
     me = lax.axis_index("rows")
     member = lax.axis_index("dim")
-    blocks, width, block_rows = unit.shape
-    fam = labels.shape[1]
+    blocks, width, block_rows = emb.shape
     rows = blocks * block_rows
-    pair = slots * block_rows
     own = rows // splits
     bar = pltpu.get_barrier_semaphore()
 
@@ -74,6 +74,15 @@
             tot_mine.at[t], tot_got.at[t, j], send_t.at[t, j], recv_t.at[t, j], dim_peer(j)
         )
 
+    def pre_copy(j):
+        return remote(pre_mine, pre_got.at[j], send_p.at[j], recv_p.at[j], dim_peer(j))
+
+    def rank_copy(k):
+        return remote(
+            ranks.at[lax.rem(me + k, groups)], rank_got.at[me], send_r.at[k], recv_r.at[k],
+            row_peer(k),
+        )
+
     def final_copy(j):
         return remote(
             fin_out.at[others[j]], out.at[member], send_f.at[j], recv_f.at[j],
@@ -85,15 +94,36 @@
     for j in range(1, splits):
         pl.semaphore_signal(bar, inc=1, device_id=dim_peer(j), device_id_type=pl.DeviceIdType.MESH)
 
-    q_all[0:width, :] = wide[...]
+    rank_got[me] = ranks[me]
+    for b in range(blocks):
+        values = emb[b]
+        pre_mine[0, b:b + 1, :] = jnp.sum(values * values, axis=0, keepdims=True)
+        pre_mine[1, b:b + 1, :] = jnp.sum(jnp.exp(prior[b]), axis=0, keepdims=True)
+    pl.semaphore_wait(bar, groups + splits - 2)
+    for k in range(1, groups):
+        rank_copy(k).start()
+    for j in range(1, splits):
+        pre_copy(j).start()
+    for j in range(1, splits):
+        pre_copy(j).wait_recv()
+    sums = pre_mine[...]
+    for j in range(1, splits):
+        sums = sums + pre_got[j]
+    scale = lax.rsqrt(sums[0] + norm_eps)
+    for b in range(blocks):
+        slices = (emb[b] * scale[b:b + 1, :]).astype(jnp.bfloat16)
+        unit[b] = slices
+        q_all[0:width, b * block_rows:(b + 1) * block_rows] = slices
+    for j in (2, 1):
+        query_copy(j).start()
+    for k in range(1, groups):
+        rank_copy(k).wait_recv()
+    down = pltpu.make_async_copy(rank_got, wanted, move.at[0])
+    down.start()
+    down.wait()
 
     def pick(k, s):
-        return wanted[lax.rem(me + k, groups), s]
-
-    for s in range(slots):
-        k_all[0, 0:width, s * block_rows:(s + 1) * block_rows] = unit[pick(0, s)]
-        near[0, 0, :, s * block_rows:(s + 1) * block_rows] = labels[pick(0, s)]
-    pl.semaphore_wait(bar, groups + splits - 2)
+        return wanted[lax.rem(me + k, groups), 0, s]
 
     @pl.loop(1, groups)
     def _(k):
@@ -101,10 +131,14 @@
             stage_u[k, :, s * block_rows:(s + 1) * block_rows] = unit[pick(k, s)]
         unit_copy(k).start()
 
-    for j in (2, 1):
-        query_copy(j).start()
+    for s in range(slots):
+        k_all[0, 0:width, s * block_rows:(s + 1) * block_rows] = unit[pick(0, s)]
     for j in (2, 1):
         key_copy(0, j).start()
+    for b in range(blocks):
+        labels[b] = (jnp.exp(prior[b]) / sums[1, b:b + 1, :]).astype(jnp.bfloat16)
+    for s in range(slots):
+        near[0, 0, :, s * block_rows:(s + 1) * block_rows] = labels[pick(0, s)]
 
     @pl.loop(1, groups)
     def _(k):
@@ -203,12 +237,14 @@
         final_copy(j).wait_recv()
         final_copy(j).wait_send()
         query_copy(j).wait_send()
+        pre_copy(j).wait_send()
         key_copy(0, j).wait_send()
         for t in range(ITERS - 1):
             total_copy(t, j).wait_send()
 
     @pl.loop(1, groups)
     def _(k):
+        rank_copy(k).wait_send()
         unit_copy(k).wait_send()
         for j in range(1, splits):
             key_copy(k, j).wait_send()
@@ -216,9 +252,9 @@
             label_copy(t, k).wait_send()
 
 
-def fused(groups, splits, slots, wanted, unit, wide, labels, seeds):
-    blocks, width, block_rows = unit.shape
-    fam = labels.shape[1]
+def fused(groups, splits, slots, ranks, emb, prior, seeds):
+    blocks, width, block_rows = emb.shape
+    fam = prior.shape[1]
     rows = blocks * block_rows
     pair = slots * block_rows
     own = rows // splits
@@ -227,9 +263,15 @@
     return pl.pallas_call(
         functools.partial(propagate, groups, splits, slots),
         out_shape=jax.ShapeDtypeStruct((splits, fam, own), jnp.float32),
-        in_specs=[pl.BlockSpec(memory_space=pltpu.SMEM)] + [vmem] * 4,
+        in_specs=[vmem] * 4,
         out_specs=vmem,
         scratch_shapes=[
+            pltpu.VMEM((blocks, width, block_rows), jnp.bfloat16),
+            pltpu.VMEM((blocks, fam, block_rows), jnp.bfloat16),
+            pltpu.VMEM((2, blocks, block_rows), jnp.float32),
+            pltpu.VMEM((splits, 2, blocks, block_rows), jnp.float32),
+            pltpu.VMEM((groups, 1, 128), jnp.int32),
+            pltpu.SMEM((groups, 1, 128), jnp.int32),
             pltpu.VMEM((splits * width, rows), jnp.bfloat16),
             pltpu.VMEM((groups, splits * width, pair), jnp.bfloat16),
             pltpu.VMEM((groups, pair, rows), jnp.float32),
@@ -248,11 +290,12 @@
             dma((groups, splits)), dma((groups, splits)),
             dma((ITERS - 1, splits)), dma((ITERS - 1, splits)),
             dma((splits,)), dma((splits,)),
+            dma((splits,)), dma((splits,)), dma((groups,)), dma((groups,)), dma((1,)),
         ],
         compiler_params=pltpu.CompilerParams(
             collective_id=0, has_side_effects=True, vmem_limit_bytes=40 * 1024 * 1024
         ),
-    )(wanted, unit, wide, labels, seeds)
+    )(ranks, emb, prior, seeds)
 
 
 def finish(mine, fam_all):
@@ -282,6 +325,17 @@
     order = jnp.sum(named.astype(jnp.int32)[:, None, :] * upto[None, :, :], axis=2) - 1
     chosen = named[:, None, :] & (order[:, None, :] == jnp.arange(slots, dtype=jnp.int32)[None, :, None])
     ranked = jnp.sum(jnp.where(chosen, places[None, None, :], 0), axis=2)
+    hot = families.reshape(blocks, 1, block_rows) - member * fam_part
+    seeds = jnp.where(
+        hot == jnp.arange(fam_part, dtype=jnp.int32)[None, :, None],
+        seed_weight * seed_mask.astype(jnp.float32).reshape(blocks, 1, block_rows),
+        0.0,
+    )
+    if shared:
+        seeds = jnp.transpose(seeds, (1, 0, 2)).reshape(fam_part, blocks * block_rows)
+        ranks = jnp.pad(ranked, ((0, 0), (0, 128 - slots)))[:, None, :]
+        mine = fused(groups, splits, slots, ranks, embeddings, prior, seeds)
+        return jnp.transpose(finish(mine.reshape(fam_all, owned * block_rows), fam_all))
     wanted = lax.all_to_all(ranked, "rows", split_axis=0, concat_axis=0, tiled=True)
     local_squares = jnp.sum(embeddings * embeddings, axis=1)
     raised_prior = jnp.exp(prior)
@@ -289,17 +343,6 @@
     squares, prior_total = lax.psum((local_squares, local_total), "dim")
     unit_blocks = (embeddings * lax.rsqrt(squares + norm_eps)[:, None, :]).astype(jnp.bfloat16)
     labels = (raised_prior / prior_total[:, None, :]).astype(jnp.bfloat16)
-    hot = families.reshape(blocks, 1, block_rows) - member * fam_part
-    seeds = jnp.where(
-        hot == jnp.arange(fam_part, dtype=jnp.int32)[None, :, None],
-        seed_weight * seed_mask.astype(jnp.float32).reshape(blocks, 1, block_rows),
-        0.0,
-    )
-    if shared:
-        wide = jnp.transpose(unit_blocks, (1, 0, 2)).reshape(width, blocks * block_rows)
-        seeds = jnp.transpose(seeds, (1, 0, 2)).reshape(fam_part, blocks * block_rows)
-        mine = fused(groups, splits, slots, wanted, unit_blocks, wide, labels, seeds)
-        return jnp.transpose(finish(mine.reshape(fam_all, owned * block_rows), fam_all))
     both = jnp.concatenate([unit_blocks, labels], axis=1)
     queries = lax.all_gather(unit_blocks, "dim", axis=1, tiled=True)
     arrived = lax.all_to_all(both[wanted], "rows", split_axis=0, concat_axis=0, tiled=True).reshape(

time: 95.6 us -> 85.9 us (0.90)
  blocking collectives: 6.32 us -> 0 us
  starting transfers between devices: 5.66 us -> 0 us
  Pallas kernels: 76.8 us -> 80.5 us
  local copies, waits for them, and re-layouts: 3.25 us -> 2.11 us
    psum x1 -> x0, blocking collectives: 6.32 us -> none  [shards(): squares, prior_total = lax.psum((local_squares, local_total), 'dim')]
    all_to_all x1 -> x0, starting transfers between devices: 5.66 us -> none  [shards(): lax.all_to_all(ranked, 'rows', split_axis=0, concat_axis=0, tiled=True)]
    pallas_call x1, Pallas kernels: 76.8 us -> 80.5 us  [fused(): pl.pallas_call(functools.partial(propagate, groups, splits, slots), out_s...]
    reduce_sum x1 -> x0, other arithmetic: 1.37 us -> none  [shards(): local_squares = jnp.sum(embeddings * embeddings, axis=1)]
    unnamed x10 -> x6, local copies, waits for them, and re-layouts: 2.27 us -> 1.72 us
  transfers between devices with their start and end apart: 1 -> 0, of which waited for: 0 -> 0; matrix products, arithmetic and copies ran while one was open for 2% -> 0% of each run, Pallas kernels for 0% -> 0%
where the time goes in v4:
time: 85.9 us; the launch traced here: 85.6 us
  Pallas kernels  80.5 us (94%)
  other arithmetic  2.94 us (3%)
  local copies, waits for them, and re-layouts  2.11 us (2%)
    pallas_call x1, Pallas kernels, fused(): pl.pallas_call(functools.partial(propagate, groups, splits, slots), out_s...  80.5 us
    unnamed x6, local copies, waits for them, and re-layouts  1.72 us

profile of v4, /device:TPU:11, one launch (start us, length us, event | category | flops | bytes accessed | tf_op | source)
XLA Modules:
  0.0 85.6 jit_solution(8461229498470602667)
XLA Ops:
  0.0 0.0 copy-start.2
  0.0 0.0 copy-start
  0.0 0.7 copy-done.2
  0.7 0.1 fusion.1
  0.8 0.1 and.11
  0.9 0.7 broadcast_subtract_fusion
  1.6 0.7 convert_multiply_fusion
  2.3 0.2 multiply_reduce_fusion.1
  2.5 0.1 select_reduce_fusion
  2.6 0.1 copy.7
  2.7 0.1 fusion.seeds
  2.8 0.0 copy-done
  2.8 0.0 copy-start.1
  2.8 1.0 %copy-done.1 = f32[8,128,128]{2,1,0:T(8,128)S(1)} copy-done((f32[8,128,128]{2,1,0:T(8,128)S(1)}, f32[8,128,128]{2,1,0:T(8,128)}, u32[]{:S(2)}) %copy-start.1) | copy-done | bytes 524312
  3.9 80.5 %shard_map.55 = f32[4,128,256]{2,1,0:T(8,128)S(1)} custom-call(s32[8,1,128]{2,1,0:T(1,128)S(1)} %bitcast.4, f32[8,128,128]{2,1,0:T(8,128)S(1)} %copy-done, f32[8,128,128]{2,1,0:T(8,128)S(1)} %copy-done.1, f32[128,1024]{1,0:T(8,128)S(1)} %fusion.seeds), custom_call_target="tpu_custom_call" | custom-call | tf_op jit(solution)/shard_map/pallas_call | solution.py:263
  84.4 0.1 multiply_reduce_fusion
  84.5 0.2 copy.8
  84.7 0.9 %add_bitcast_fusion = f32[256,512]{1,0:T(8,128)} fusion(f32[512,256]{0,1:T(8,128)S(1)} %copy.8, f32[256]{0:T(256)S(1)} %log.13), kind=kLoop, calls=%fused_computation | loop fusion | flops 262144 | bytes 1049600 | tf_op jit(solution)/shard_map/transpose | solution.py:338
  (5 shorter events, 0.0 us)
Async XLA Ops:
  0.0 0.7 copy-start.2
  0.0 2.8 %copy-start = (f32[8,128,128]{2,1,0:T(8,128)S(1)}, f32[8,128,128]{2,1,0:T(8,128)}, u32[]{:S(2)}) copy-start(f32[8,128,128]{2,1,0:T(8,128)} %emb.1) | copy-start | bytes 1572868
  2.8 1.0 %copy-start.1 = (f32[8,128,128]{2,1,0:T(8,128)S(1)}, f32[8,128,128]{2,1,0:T(8,128)}, u32[]{:S(2)}) copy-start(f32[8,128,128]{2,1,0:T(8,128)} %prior.1) | copy-start | bytes 1572868

commit v5 on v4

--- a/solution.py
+++ b/solution.py
@@ -20,7 +20,7 @@
     groups, splits, slots,
     ranks, emb, prior, seeds, out,
     unit, labels, pre_mine, pre_got, rank_got, wanted,
-    q_all, k_all, raw, w_all, near, stage_u, stage_l, mixed, fresh, tot_mine, tot_got, fin_out,
+    q_all, k_all, turned, raw, w_all, near, stage_u, stage_l, mixed, fresh, tot_mine, tot_got, fin_out,
     send_u, recv_u, send_l, recv_l, send_q, recv_q, send_k, recv_k, send_t, recv_t, send_f, recv_f,
     send_p, recv_p, send_r, recv_r, move,
 ):
@@ -144,7 +144,6 @@
     def _(k):
         for s in range(slots):
             stage_l[0, k, :, s * block_rows:(s + 1) * block_rows] = labels[pick(k, s)]
-        label_copy(0, k).start()
 
     query_copy(2).wait_recv()
     query_copy(3).start()
@@ -155,12 +154,13 @@
     def score(k):
         key_copy(k, 1).wait_recv()
         key_copy(k, 3).wait_recv()
+        turned[...] = k_all[k].T
 
         @pl.loop(0, splits)
         def _(c):
             cols = pl.ds(pl.multiple_of(c * own, own), own)
             cosine = lax.dot_general(
-                k_all[k], q_all[:, cols], (((0,), (0,)), ((), ())),
+                turned[...], q_all[:, cols], (((1,), (0,)), ((), ())),
                 preferred_element_type=jnp.float32,
             )
             raised = jnp.exp(sharpness * (cosine - 1.0))
@@ -171,6 +171,7 @@
         unit_copy(k).wait_recv()
         key_copy(k, 2).start()
         key_copy(k, 1).start()
+        label_copy(0, k).start()
 
     def hand_on(k):
         key_copy(k, 2).wait_recv()
@@ -274,6 +275,7 @@
             pltpu.SMEM((groups, 1, 128), jnp.int32),
             pltpu.VMEM((splits * width, rows), jnp.bfloat16),
             pltpu.VMEM((groups, splits * width, pair), jnp.bfloat16),
+            pltpu.VMEM((pair, splits * width), jnp.bfloat16),
             pltpu.VMEM((groups, pair, rows), jnp.float32),
             pltpu.VMEM((groups, pair, rows), jnp.bfloat16),
             pltpu.VMEM((ITERS, groups, fam, pair), jnp.bfloat16),

time: 85.9 us -> 84.6 us (0.985)
  Pallas kernels: 80.5 us -> 79.2 us
    pallas_call x1, Pallas kernels: 80.5 us -> 79.2 us  [fused(): pl.pallas_call(functools.partial(propagate, groups, splits, slots), out_s...]
where the time goes in v5:
time: 84.6 us; the launch traced here: 84.3 us
  Pallas kernels  79.2 us (94%)
  other arithmetic  2.94 us (3%)
  local copies, waits for them, and re-layouts  2.11 us (2%)
    pallas_call x1, Pallas kernels, fused(): pl.pallas_call(functools.partial(propagate, groups, splits, slots), out_s...  79.2 us
    unnamed x6, local copies, waits for them, and re-layouts  1.72 us

profile of v5, /device:TPU:11, one launch (start us, length us, event | category | flops | bytes accessed | tf_op | source)
XLA Modules:
  0.0 84.3 jit_solution(542675004014219397)
XLA Ops:
  0.0 0.0 copy-start.2
  0.0 0.0 copy-start
  0.0 0.7 copy-done.2
  0.7 0.1 fusion.1
  0.8 0.1 and.11
  0.9 0.7 broadcast_subtract_fusion
  1.6 0.7 convert_multiply_fusion
  2.3 0.2 multiply_reduce_fusion.1
  2.5 0.1 select_reduce_fusion
  2.6 0.1 copy.7
  2.7 0.1 fusion.seeds
  2.8 0.0 copy-done
  2.8 0.0 copy-start.1
  2.8 1.0 %copy-done.1 = f32[8,128,128]{2,1,0:T(8,128)S(1)} copy-done((f32[8,128,128]{2,1,0:T(8,128)S(1)}, f32[8,128,128]{2,1,0:T(8,128)}, u32[]{:S(2)}) %copy-start.1) | copy-done | bytes 524312
  3.9 79.2 %shard_map.55 = f32[4,128,256]{2,1,0:T(8,128)S(1)} custom-call(s32[8,1,128]{2,1,0:T(1,128)S(1)} %bitcast.4, f32[8,128,128]{2,1,0:T(8,128)S(1)} %copy-done, f32[8,128,128]{2,1,0:T(8,128)S(1)} %copy-done.1, f32[128,1024]{1,0:T(8,128)S(1)} %fusion.seeds), custom_call_target="tpu_custom_call" | custom-call | tf_op jit(solution)/shard_map/pallas_call | solution.py:264
  83.1 0.1 multiply_reduce_fusion
  83.2 0.2 copy.8
  83.4 0.9 %add_bitcast_fusion = f32[256,512]{1,0:T(8,128)} fusion(f32[512,256]{0,1:T(8,128)S(1)} %copy.8, f32[256]{0:T(256)S(1)} %log.13), kind=kLoop, calls=%fused_computation | loop fusion | flops 262144 | bytes 1049600 | tf_op jit(solution)/shard_map/transpose | solution.py:340
  (5 shorter events, 0.0 us)
Async XLA Ops:
  0.0 0.7 copy-start.2
  0.0 2.8 %copy-start = (f32[8,128,128]{2,1,0:T(8,128)S(1)}, f32[8,128,128]{2,1,0:T(8,128)}, u32[]{:S(2)}) copy-start(f32[8,128,128]{2,1,0:T(8,128)} %emb.1) | copy-start | bytes 1572868
  2.8 1.0 %copy-start.1 = (f32[8,128,128]{2,1,0:T(8,128)S(1)}, f32[8,128,128]{2,1,0:T(8,128)}, u32[]{:S(2)}) copy-start(f32[8,128,128]{2,1,0:T(8,128)} %prior.1) | copy-start | bytes 1572868

commit v6 on v5

--- a/solution.py
+++ b/solution.py
@@ -18,7 +18,8 @@
 
 def propagate(
     groups, splits, slots,
-    ranks, emb, prior, seeds, out,
+    ranks, emb, prior, known, kinds, out,
+    seeds,
     unit, labels, pre_mine, pre_got, rank_got, wanted,
     q_all, k_all, turned, raw, w_all, near, stage_u, stage_l, mixed, fresh, tot_mine, tot_got, fin_out,
     send_u, recv_u, send_l, recv_l, send_q, recv_q, send_k, recv_k, send_t, recv_t, send_f, recv_f,
@@ -145,6 +146,10 @@
         for s in range(slots):
             stage_l[0, k, :, s * block_rows:(s + 1) * block_rows] = labels[pick(k, s)]
 
+    family = lax.broadcasted_iota(jnp.int32, seeds.shape, 0) + member * seeds.shape[0]
+    seeds[...] = jnp.where(
+        kinds[...] == family, seed_weight * known[...].astype(jnp.float32), 0.0
+    )
     query_copy(2).wait_recv()
     query_copy(3).start()
     query_copy(1).wait_recv()
@@ -253,7 +258,7 @@
             label_copy(t, k).wait_send()
 
 
-def fused(groups, splits, slots, ranks, emb, prior, seeds):
+def fused(groups, splits, slots, ranks, emb, prior, known, kinds):
     blocks, width, block_rows = emb.shape
     fam = prior.shape[1]
     rows = blocks * block_rows
@@ -264,9 +269,10 @@
     return pl.pallas_call(
         functools.partial(propagate, groups, splits, slots),
         out_shape=jax.ShapeDtypeStruct((splits, fam, own), jnp.float32),
-        in_specs=[vmem] * 4,
+        in_specs=[vmem] * 5,
         out_specs=vmem,
         scratch_shapes=[
+            pltpu.VMEM((fam, rows), jnp.float32),
             pltpu.VMEM((blocks, width, block_rows), jnp.bfloat16),
             pltpu.VMEM((blocks, fam, block_rows), jnp.bfloat16),
             pltpu.VMEM((2, blocks, block_rows), jnp.float32),
@@ -297,7 +303,7 @@
         compiler_params=pltpu.CompilerParams(
             collective_id=0, has_side_effects=True, vmem_limit_bytes=40 * 1024 * 1024
         ),
-    )(ranks, emb, prior, seeds)
+    )(ranks, emb, prior, known, kinds)
 
 
 def finish(mine, fam_all):
@@ -327,17 +333,16 @@
     order = jnp.sum(named.astype(jnp.int32)[:, None, :] * upto[None, :, :], axis=2) - 1
     chosen = named[:, None, :] & (order[:, None, :] == jnp.arange(slots, dtype=jnp.int32)[None, :, None])
     ranked = jnp.sum(jnp.where(chosen, places[None, None, :], 0), axis=2)
+    if shared:
+        ranks = jnp.pad(ranked, ((0, 0), (0, 128 - slots)))[:, None, :]
+        mine = fused(groups, splits, slots, ranks, embeddings, prior, seed_mask[None, :], families[None, :])
+        return jnp.transpose(finish(mine.reshape(fam_all, owned * block_rows), fam_all))
     hot = families.reshape(blocks, 1, block_rows) - member * fam_part
     seeds = jnp.where(
         hot == jnp.arange(fam_part, dtype=jnp.int32)[None, :, None],
         seed_weight * seed_mask.astype(jnp.float32).reshape(blocks, 1, block_rows),
         0.0,
     )
-    if shared:
-        seeds = jnp.transpose(seeds, (1, 0, 2)).reshape(fam_part, blocks * block_rows)
-        ranks = jnp.pad(ranked, ((0, 0), (0, 128 - slots)))[:, None, :]
-        mine = fused(groups, splits, slots, ranks, embeddings, prior, seeds)
-        return jnp.transpose(finish(mine.reshape(fam_all, owned * block_rows), fam_all))
     wanted = lax.all_to_all(ranked, "rows", split_axis=0, concat_axis=0, tiled=True)
     local_squares = jnp.sum(embeddings * embeddings, axis=1)
     raised_prior = jnp.exp(prior)

time: 84.6 us -> 84.8 us (level)
  local copies, waits for them, and re-layouts: 2.11 us -> 3.17 us
    unnamed x6 -> x8, local copies, waits for them, and re-layouts: 1.72 us -> 2.78 us
where the time goes in v6:
time: 84.8 us; the launch traced here: 84.6 us
  Pallas kernels  79.2 us (93%)
  local copies, waits for them, and re-layouts  3.17 us (4%)
  other arithmetic  2.19 us (3%)
    pallas_call x1, Pallas kernels, fused(): pl.pallas_call(functools.partial(propagate, groups, splits, slots), out_s...  79.2 us
    unnamed x8, local copies, waits for them, and re-layouts  2.78 us

profile of v6, /device:TPU:11, one launch (start us, length us, event | category | flops | bytes accessed | tf_op | source)
XLA Modules:
  0.0 84.6 jit_solution(17964214584262632951)
XLA Ops:
  0.0 0.8 fusion
  0.8 0.1 and.10
  0.9 0.2 multiply_reduce_fusion.1
  1.1 0.1 select_reduce_fusion
  1.3 0.1 copy.7
  1.4 0.0 copy-start.2
  1.4 0.0 copy-start.3
  1.4 0.7 copy-done.2
  2.1 0.0 copy-done.3
  2.1 0.0 copy-start
  2.1 1.0 %copy-done = f32[8,128,128]{2,1,0:T(8,128)S(1)} copy-done((f32[8,128,128]{2,1,0:T(8,128)S(1)}, f32[8,128,128]{2,1,0:T(8,128)}, u32[]{:S(2)}) %copy-start) | copy-done | bytes 524312
  3.1 0.0 copy-start.1
  3.1 1.0 %copy-done.1 = f32[8,128,128]{2,1,0:T(8,128)S(1)} copy-done((f32[8,128,128]{2,1,0:T(8,128)S(1)}, f32[8,128,128]{2,1,0:T(8,128)}, u32[]{:S(2)}) %copy-start.1) | copy-done | bytes 524312
  4.2 79.2 %shard_map.55 = f32[4,128,256]{2,1,0:T(8,128)S(1)} custom-call(s32[8,1,128]{2,1,0:T(1,128)S(1)} %bitcast.6, f32[8,128,128]{2,1,0:T(8,128)S(1)} %copy-done, f32[8,128,128]{2,1,0:T(8,128)S(1)} %copy-done.1, s32[1,1024]{1,0:T(1,128)S(1)} %bitcast.7, s32[1,1024]{1,0:T(1,128)S(1)} %bitcast.8), custom_call_target="tpu_custom_call" | custom-call | tf_op jit(solution)/shard_map/pallas_call | solution.py:269
  83.3 0.1 multiply_reduce_fusion
  83.5 0.2 copy.8
  83.7 0.9 %add_bitcast_fusion = f32[256,512]{1,0:T(8,128)} fusion(f32[512,256]{0,1:T(8,128)S(1)} %copy.8, f32[256]{0:T(256)S(1)} %log.13), kind=kLoop, calls=%fused_computation | loop fusion | flops 262144 | bytes 1049600 | tf_op jit(solution)/shard_map/transpose | solution.py:339
  (5 shorter events, 0.0 us)
Async XLA Ops:
  1.4 0.7 copy-start.2
  1.4 0.7 copy-start.3
  2.1 1.0 %copy-start = (f32[8,128,128]{2,1,0:T(8,128)S(1)}, f32[8,128,128]{2,1,0:T(8,128)}, u32[]{:S(2)}) copy-start(f32[8,128,128]{2,1,0:T(8,128)} %emb.1) | copy-start | bytes 1572868
  3.1 1.0 %copy-start.1 = (f32[8,128,128]{2,1,0:T(8,128)S(1)}, f32[8,128,128]{2,1,0:T(8,128)}, u32[]{:S(2)}) copy-start(f32[8,128,128]{2,1,0:T(8,128)} %prior.1) | copy-start | bytes 1572868
